TPU v7x, 256 devices: a whole 4x4x8 slice. The times are simulated.
256 devices in a mesh: frame: 64 (over z, y, core), head: 4 (over x).
Axes of the slice: x: 4, y: 4, z: 8, core: 2. Of those that a mesh axis runs over, the one named last changes fastest.
Arguments:
- qk: bfloat16 [24576, 3072], P(('frame', 'head')), may hold values from -5 to 5
- value: bfloat16 [24576, 3072], P(('frame', 'head')), may hold values from -6 to 6
- pair_mask: int32 [64, 3], P('frame'), may hold values 0 or 1
Outputs:
- attended: bfloat16 [24576, 3072], P(('frame', 'head'))
All inputs are finite; a program needn't handle non-finite values. No bound on the sum of `pair_mask` on one device may be relied on, other than what follows from the above.
Results may differ from a plain program's by a relative error of at most 0.0045.
Values may be sent and summed in bfloat16 or wider, within the bound.
A program may use at most 64 MiB of HBM per device.

v0:
```python
import math

import jax
import jax.numpy as jnp
from jax import lax
from jax.sharding import PartitionSpec as P

DH = 128


def from_behind(value, axis, steps):
    count = lax.axis_size(axis)
    first, last = (max(0, -steps), min(count, count - steps))
    return lax.ppermute(value, axis, [(source, source + steps) for source in range(first, last)])


def pair_tile(rows_qk, cols_qk, rows_value, cols_value, skip_self, with_columns):
    heads = rows_qk.shape[1] // DH
    scale = 1.0 / math.sqrt(DH)
    row_maxima, row_sums, row_outs = ([], [], [])
    col_maxima, col_sums, col_outs = ([], [], [])
    for index_head in range(heads):
        start = index_head * DH
        left = rows_qk[:, start : start + DH]
        right = cols_qk[:, start : start + DH]
        scores = (
            lax.dot_general(
                left, right, (((1,), (1,)), ((), ())), preferred_element_type=jnp.float32
            )
            * scale
        )
        if skip_self:
            first = lax.broadcasted_iota(jnp.int32, scores.shape, 0)
            second = lax.broadcasted_iota(jnp.int32, scores.shape, 1)
            scores = jnp.where(first == second, -jnp.inf, scores)
        row_max = jnp.max(scores, axis=1)
        weights = jnp.exp(scores - row_max[:, None])
        row_maxima.append(row_max)
        row_sums.append(jnp.sum(weights, axis=1))
        row_outs.append(
            jnp.dot(
                weights.astype(jnp.bfloat16),
                cols_value[:, start : start + DH],
                preferred_element_type=jnp.float32,
            )
        )
        if with_columns:
            col_max = jnp.max(scores, axis=0)
            col_weights = jnp.exp(scores - col_max[None, :])
            col_maxima.append(col_max)
            col_sums.append(jnp.sum(col_weights, axis=0))
            col_outs.append(
                lax.dot_general(
                    col_weights.astype(jnp.bfloat16),
                    rows_value[:, start : start + DH],
                    (((0,), (0,)), ((), ())),
                    preferred_element_type=jnp.float32,
                )
            )
    row_part = (jnp.stack(row_maxima, 1), jnp.stack(row_sums, 1), jnp.stack(row_outs, 1))
    if with_columns:
        return (
            row_part,
            (jnp.stack(col_maxima, 1), jnp.stack(col_sums, 1), jnp.stack(col_outs, 1)),
        )
    return row_part


def absorb(state, part):
    best, total, numerator = state
    other_max, other_sum, other_out = part
    alive = other_sum > 0.0
    newest = jnp.where(alive, jnp.maximum(best, other_max), best)
    keep = jnp.exp(best - newest)
    take = jnp.where(alive, jnp.exp(jnp.minimum(other_max - newest, 0.0)), 0.0)
    return (
        newest,
        total * keep + other_sum * take,
        numerator * keep[:, :, None] + other_out * take[:, :, None],
    )


def local(qk, value, pair_mask):
    qk_heads, value_heads = (
        lax.all_to_all(qk, "head", split_axis=1, concat_axis=0, tiled=True),
        lax.all_to_all(value, "head", split_axis=1, concat_axis=0, tiled=True),
    )
    frames = lax.axis_size("frame")
    place = lax.axis_index("frame")
    tokens_here = qk_heads.shape[0]
    heads = qk_heads.shape[1] // DH
    reach = pair_mask.shape[1]
    mask_row = pair_mask[0]
    empty = (
        jnp.zeros((tokens_here, heads), jnp.float32),
        jnp.zeros((tokens_here, heads), jnp.float32),
        jnp.zeros((tokens_here, heads, DH), jnp.float32),
    )
    state = pair_tile(qk_heads, qk_heads, value_heads, value_heads, True, False)
    for offset in range(1, reach + 1):
        upper_qk, upper_value = from_behind((qk_heads, value_heads), "frame", -offset)
        live_up = (mask_row[offset - 1] == 1) & (place + offset < frames)
        row_part, col_part = lax.cond(
            live_up,
            lambda: pair_tile(qk_heads, upper_qk, value_heads, upper_value, False, True),
            lambda: (empty, empty),
        )
        state = absorb(state, row_part)
        returned = from_behind(col_part, "frame", offset)
        state = absorb(state, returned)
    best, total, numerator = state
    attended = (numerator / total[:, :, None]).astype(jnp.bfloat16).reshape(tokens_here, heads * DH)
    return lax.all_to_all(attended, "head", split_axis=0, concat_axis=1, tiled=True)


def solution(mesh):
    return jax.shard_map(
        local,
        mesh=mesh,
        in_specs=(P(("frame", "head"), None), P(("frame", "head"), None), P("frame", None)),
        out_specs=P(("frame", "head"), None),
        check_vma=False,
    )
```

profile of v0, /device:TPU:64, one launch (start us, length us, event | category | flops | bytes accessed | tf_op | source)
XLA Modules:
  0.0 322.9 jit_solution(772956289406347488)
XLA Ops:
  0.0 2.0 copy.32
  2.0 4.3 %all-to-all-start = ((bf16[96,4,768]{2,0,1:T(8,128)(2,1)}), bf16[96,4,768]{2,0,1:T(8,128)(2,1)S(1)}, u32[]{:S(2)}, u32[]{:S(2)}) async-start(bf16[96,4,768]{2,0,1:T(8,128)(2,1)} %bitcast.187), calls=%async_computation | async-start | bytes 1179648 | tf_op jit(solution)/shard_map/all_to_all | solution.py:85
  7.1 9.3 %all-to-all-done = bf16[96,4,768]{2,0,1:T(8,128)(2,1)S(1)} async-done(((bf16[96,4,768]{2,0,1:T(8,128)(2,1)}), bf16[96,4,768]{2,0,1:T(8,128)(2,1)S(1)}, u32[]{:S(2)}, u32[]{:S(2)}) %all-to-all-start) | async-done | bytes 589856 | tf_op jit(solution)/shard_map/all_to_all | solution.py:85
  16.5 3.5 %all-to-all-start.1 = ((bf16[96,4,768]{2,0,1:T(8,128)(2,1)}), bf16[96,4,768]{2,0,1:T(8,128)(2,1)S(1)}, u32[]{:S(2)}, u32[]{:S(2)}) async-start(bf16[96,4,768]{2,0,1:T(8,128)(2,1)} %bitcast.186), calls=%async_computation.1 | async-start | bytes 1179648 | tf_op jit(solution)/shard_map/all_to_all | solution.py:86
  22.5 2.9 collective-permute-start.10
  25.4 3.5 %collective-permute-start.5 = (bf16[384,768]{1,0:T(8,128)(2,1)S(1)}, bf16[384,768]{1,0:T(8,128)(2,1)}, u32[]{:S(2)}, u32[]{:S(2)}) collective-permute-start(bf16[384,768]{1,0:T(8,128)(2,1)S(1)} %bitcast.201), channel_id=1, source_target_pairs={{8,0},{12,4},{16,8},{20,12},{24,16},{28,20},{32,24},{36,28},{40,32... | collective-permute-start | bytes 1769480 | tf_op jit(solution)/shard_map/ppermute | solution.py:14
  29.2 2.2 collective-permute-start.11
  31.3 5.1 %collective-permute-start.6 = (bf16[384,768]{1,0:T(8,128)(2,1)S(1)}, bf16[384,768]{1,0:T(8,128)(2,1)}, u32[]{:S(2)}, u32[]{:S(2)}) collective-permute-start(bf16[384,768]{1,0:T(8,128)(2,1)S(1)} %bitcast.189), channel_id=1, source_target_pairs={{8,0},{12,4},{16,8},{20,12},{24,16},{28,20},{32,24},{36,28},{40,32... | collective-permute-start | bytes 1769480 | tf_op jit(solution)/shard_map/ppermute | solution.py:14
  36.4 1.9 collective-permute-start
  42.8 8.2 %collective-permute-done.10 = bf16[384,768]{1,0:T(8,128)(2,1)S(1)} collective-permute-done((bf16[384,768]{1,0:T(8,128)(2,1)S(1)}, bf16[384,768]{1,0:T(8,128)(2,1)S(1)}, u32[]{:S(2)}, u32[]{:S(2)}) %collective-permute-start.10) | collective-permute-done | bytes 589856 | tf_op jit(solution)/shard_map/ppermute | solution.py:14
  50.9 1.9 collective-permute-start.1
  54.1 22.2 %collective-permute-done.11 = bf16[384,768]{1,0:T(8,128)(2,1)} collective-permute-done((bf16[384,768]{1,0:T(8,128)(2,1)S(1)}, bf16[384,768]{1,0:T(8,128)(2,1)}, u32[]{:S(2)}, u32[]{:S(2)}) %collective-permute-start.11) | collective-permute-done | bytes 589856 | tf_op jit(solution)/shard_map/ppermute | solution.py:14
  76.3 55.7 %conditional.5 = (f32[384,6]{0,1:T(8,128)S(1)}, f32[384,6]{0,1:T(8,128)S(1)}, f32[384,6,128]{2,0,1:T(8,128)S(1)}, f32[384,6]{0,1:T(8,128)}, f32[384,6]{0,1:T(8,128)}, /*index=5*/f32[384,6,128]{2,0,1:T(8,128)}) conditional(s32[]{:T(128)} %convert_element_type.146, () %tuple.33, (bf16[384,768]{1,0:T(8,128)(2,1)S(1)}, ...), branch_computations={%region_58.59_spmd, %region_59.84_spmd} | conditional | flops 689200128 | bytes 45233100 | solution.py:103
  80.2 1.8 fusion.320
  82.5 2.5 fusion.319
  85.6 2.5 fusion.318
  90.1 1.6 fusion.193
  92.2 1.6 fusion.195
  94.4 1.5 fusion.197
  125.6 1.7 fusion.172
  127.3 1.7 fusion.171
  132.0 1.9 collective-permute-start.14
  134.0 59.2 %conditional.4 = (f32[384,6]{0,1:T(8,128)S(1)}, f32[384,6]{0,1:T(8,128)}, f32[384,6,128]{2,0,1:T(8,128)S(1)}, f32[384,6]{0,1:T(8,128)}, f32[384,6]{0,1:T(8,128)}, /*index=5*/f32[384,6,128]{2,0,1:T(8,128)}) conditional(s32[]{:T(128)} %convert_element_type.145, () %tuple.31, (bf16[384,768]{1,0:T(8,128)(2,1)S(1)}, bf16[384,768]{1,0:T(8,128)(2,1)}, ...), branch_computations={%region_32.0_spmd, %region_33.58_spmd} | conditional | flops 689200128 | bytes 42830712 | solution.py:103
  136.0 1.8 fusion.316
  138.9 1.8 fusion.315
  141.9 1.8 fusion.314
  144.2 2.6 fusion.313
  147.3 2.6 fusion.312
  151.8 1.6 fusion.109
  153.9 1.6 fusion.111
  186.9 1.6 fusion.88
  188.6 1.7 fusion.87
  193.2 1.9 collective-permute-start.9
  195.2 63.9 %conditional.3 = (f32[384,6]{0,1:T(8,128)}, f32[384,6]{0,1:T(8,128)}, f32[384,6,128]{2,0,1:T(8,128)}, f32[384,6]{0,1:T(8,128)}, f32[384,6]{0,1:T(8,128)}, /*index=5*/f32[384,6,128]{2,0,1:T(8,128)}) conditional(s32[]{:T(128)} %convert_element_type.144, () %tuple.29, (bf16[384,768]{1,0:T(8,128)(2,1)S(1)}, bf16[384,768]{1,0:T(8,128)(2,1)}, ...), branch_computations={%region_6.7_spmd, %region_7.32_spmd} | conditional | flops 689200128 | bytes 33391936 | solution.py:103
  197.8 1.8 fusion.310
  200.8 1.8 fusion.309
  203.7 1.8 fusion.308
  206.1 2.6 fusion.307
  209.2 2.6 fusion.306
  214.3 1.6 fusion.25
  216.5 1.6 fusion.27
  218.6 1.5 fusion.29
  220.8 1.5 fusion.31
  226.9 1.9 fusion.11
  228.8 1.9 fusion.10
  230.7 1.9 fusion.9
  232.7 1.9 fusion.8
  234.5 1.9 fusion.7
  236.4 1.9 fusion.6
  252.8 1.6 fusion.4
  254.4 1.7 fusion.3
  259.1 2.0 collective-permute-start.4
  262.5 1.9 collective-permute-start.7
  264.4 1.9 collective-permute-start.2
  266.5 4.1 %collective-permute-done.7 = f32[384,6]{0,1:T(8,128)S(1)} collective-permute-done((f32[384,6]{0,1:T(8,128)}, f32[384,6]{0,1:T(8,128)S(1)}, u32[]{:S(2)}, u32[]{:S(2)}) %collective-permute-start.7) | collective-permute-done | bytes 9248 | tf_op jit(solution)/shard_map/ppermute | solution.py:14
  270.6 1.9 collective-permute-start.8
  272.5 7.0 %collective-permute-done.2 = f32[384,6]{0,1:T(8,128)S(1)} collective-permute-done((f32[384,6]{0,1:T(8,128)}, f32[384,6]{0,1:T(8,128)S(1)}, u32[]{:S(2)}, u32[]{:S(2)}) %collective-permute-start.2) | collective-permute-done | bytes 9248 | tf_op jit(solution)/shard_map/ppermute | solution.py:14
  279.6 3.8 %collective-permute-start.3 = (f32[384,6]{0,1:T(8,128)}, f32[384,6]{0,1:T(8,128)S(1)}, u32[]{:S(2)}, u32[]{:S(2)}) collective-permute-start(f32[384,6]{0,1:T(8,128)} %get-tuple-element.63), channel_id=1, source_target_pairs={{0,4},{4,8},{8,12},{12,16},{16,20},{20,24},{24,28},{28,32},{32,36}... | collective-permute-start | bytes 27656 | tf_op jit(solution)/shard_map/ppermute | solution.py:14
  283.8 2.2 collective-permute-start.12
  286.0 2.4 collective-permute-done.3
  288.4 1.9 collective-permute-start.13
  291.2 4.6 %collective-permute-done.13 = f32[384,6]{0,1:T(8,128)S(1)} collective-permute-done((f32[384,6]{0,1:T(8,128)S(1)}, f32[384,6]{0,1:T(8,128)S(1)}, u32[]{:S(2)}, u32[]{:S(2)}) %collective-permute-start.13) | collective-permute-done | bytes 9248 | tf_op jit(solution)/shard_map/ppermute | solution.py:14
  296.6 9.5 %divide_convert_fusion = bf16[384,6,128]{2,0,1:T(8,128)(2,1)S(1)} fusion(f32[384,6,128]{2,0,1:T(8,128)} %collective-permute-done.14, f32[384,6,128]{2,0,1:T(8,128)S(1)} %copy-done.21, f32[384,6,128]{2,0,1:T(8,128)} %collective-permute-done.9, f32[384,6,128]{2,0,1:T(8,128)S(1)} %copy-done.25, f32[384,6,128]{2,0,1:T(8,128)} %collective-permute-done.4, ...), kind=kLoop, calls=%fused_computation.318 | loop fusion | flops 5898240 | bytes 8967168 | tf_op jit(solution)/shard_map/convert_element_type | solution.py:112
  307.3 14.8 %all_to_all.57 = bf16[4,96,768]{2,1,0:T(8,128)(2,1)S(1)} all-to-all(bf16[4,96,768]{2,1,0:T(8,128)(2,1)S(1)} %all_to_all.50), channel_id=1, replica_groups=mesh['frame'=64,'head'=4] {'head'}, dimensions={0} | all-to-all | bytes 1179648 | tf_op jit(solution)/shard_map/all_to_all | solution.py:113
  (411 shorter events, 127.0 us)
Async XLA Ops:
  2.0 14.5 %all-to-all-start = ((bf16[96,4,768]{2,0,1:T(8,128)(2,1)}), bf16[96,4,768]{2,0,1:T(8,128)(2,1)S(1)}, u32[]{:S(2)}, u32[]{:S(2)}) async-start(bf16[96,4,768]{2,0,1:T(8,128)(2,1)} %bitcast.187), calls=%async_computation | async-start | bytes 1179648 | tf_op jit(solution)/shard_map/all_to_all | solution.py:85
  6.3 13.7 %copy-start.119 = (s32[1,3]{1,0:T(1,128)S(1)}, s32[1,3]{1,0:T(1,128)}, u32[]{:S(2)}) copy-start(s32[1,3]{1,0:T(1,128)} %param.11) | copy-start | bytes 40
  16.5 12.7 %all-to-all-start.1 = ((bf16[96,4,768]{2,0,1:T(8,128)(2,1)}), bf16[96,4,768]{2,0,1:T(8,128)(2,1)S(1)}, u32[]{:S(2)}, u32[]{:S(2)}) async-start(bf16[96,4,768]{2,0,1:T(8,128)(2,1)} %bitcast.186), calls=%async_computation.1 | async-start | bytes 1179648 | tf_op jit(solution)/shard_map/all_to_all | solution.py:86
  22.5 28.4 %collective-permute-start.10 = (bf16[384,768]{1,0:T(8,128)(2,1)S(1)}, bf16[384,768]{1,0:T(8,128)(2,1)S(1)}, u32[]{:S(2)}, u32[]{:S(2)}) collective-permute-start(bf16[384,768]{1,0:T(8,128)(2,1)S(1)} %bitcast.200), channel_id=1, source_target_pairs={{12,0},{16,4},{20,8},{24,12},{28,16},{32,20},{36,24},{40,28},{44,3... | collective-permute-start | bytes 1769480 | tf_op jit(solution)/shard_map/ppermute | solution.py:14
  25.4 108.5 %collective-permute-start.5 = (bf16[384,768]{1,0:T(8,128)(2,1)S(1)}, bf16[384,768]{1,0:T(8,128)(2,1)}, u32[]{:S(2)}, u32[]{:S(2)}) collective-permute-start(bf16[384,768]{1,0:T(8,128)(2,1)S(1)} %bitcast.201), channel_id=1, source_target_pairs={{8,0},{12,4},{16,8},{20,12},{24,16},{28,20},{32,24},{36,28},{40,32... | collective-permute-start | bytes 1769480 | tf_op jit(solution)/shard_map/ppermute | solution.py:14
  29.2 47.1 %collective-permute-start.11 = (bf16[384,768]{1,0:T(8,128)(2,1)S(1)}, bf16[384,768]{1,0:T(8,128)(2,1)}, u32[]{:S(2)}, u32[]{:S(2)}) collective-permute-start(bf16[384,768]{1,0:T(8,128)(2,1)S(1)} %bitcast.188), channel_id=1, source_target_pairs={{12,0},{16,4},{20,8},{24,12},{28,16},{32,20},{36,24},{40,28},{44,3... | collective-permute-start | bytes 1769480 | tf_op jit(solution)/shard_map/ppermute | solution.py:14
  31.3 102.6 %collective-permute-start.6 = (bf16[384,768]{1,0:T(8,128)(2,1)S(1)}, bf16[384,768]{1,0:T(8,128)(2,1)}, u32[]{:S(2)}, u32[]{:S(2)}) collective-permute-start(bf16[384,768]{1,0:T(8,128)(2,1)S(1)} %bitcast.189), channel_id=1, source_target_pairs={{8,0},{12,4},{16,8},{20,12},{24,16},{28,20},{32,24},{36,28},{40,32... | collective-permute-start | bytes 1769480 | tf_op jit(solution)/shard_map/ppermute | solution.py:14
  36.4 158.7 %collective-permute-start = (bf16[384,768]{1,0:T(8,128)(2,1)S(1)}, bf16[384,768]{1,0:T(8,128)(2,1)}, u32[]{:S(2)}, u32[]{:S(2)}) collective-permute-start(bf16[384,768]{1,0:T(8,128)(2,1)S(1)} %bitcast.202), channel_id=1, source_target_pairs={{4,0},{8,4},{12,8},{16,12},{20,16},{24,20},{28,24},{32,28},{36,32}... | collective-permute-start | bytes 1769480 | tf_op jit(solution)/shard_map/ppermute | solution.py:14
  39.5 14.0 %copy-start.109 = (f32[384]{0:T(512)}, f32[384]{0:T(512)S(1)}, u32[]{:S(2)}) copy-start(f32[384]{0:T(512)S(1)} %get-tuple-element.195) | copy-start | bytes 4612
  39.8 14.0 %copy-start.26 = (f32[384,384]{0,1:T(8,128)}, f32[384,384]{0,1:T(8,128)S(1)}, u32[]{:S(2)}) copy-start(f32[384,384]{0,1:T(8,128)S(1)} %get-tuple-element.198) | copy-start | bytes 1769476
  39.8 14.0 %copy-start.111 = (f32[384]{0:T(512)}, f32[384]{0:T(512)S(1)}, u32[]{:S(2)}) copy-start(f32[384]{0:T(512)S(1)} %get-tuple-element.197) | copy-start | bytes 4612
  50.9 144.2 %collective-permute-start.1 = (bf16[384,768]{1,0:T(8,128)(2,1)S(1)}, bf16[384,768]{1,0:T(8,128)(2,1)}, u32[]{:S(2)}, u32[]{:S(2)}) collective-permute-start(bf16[384,768]{1,0:T(8,128)(2,1)S(1)} %bitcast.193), channel_id=1, source_target_pairs={{4,0},{8,4},{12,8},{16,12},{20,16},{24,20},{28,24},{32,28},{36,32}... | collective-permute-start | bytes 1769480 | tf_op jit(solution)/shard_map/ppermute | solution.py:14
  54.1 22.2 %copy-start.28 = (f32[384,6,128]{2,0,1:T(8,128)}, f32[384,6,128]{2,0,1:T(8,128)S(1)}, u32[]{:S(2)}) copy-start(f32[384,6,128]{2,0,1:T(8,128)S(1)} %fusion.259) | copy-start | bytes 3538948
  79.6 8.5 %copy-start.72 = (f32[384]{0:T(512)}, f32[384]{0:T(512)S(1)}, u32[]{:S(2)}) copy-start(f32[384]{0:T(512)S(1)} %get-tuple-element.144) | copy-start | bytes 4612 | tf_op jit(solution)/shard_map/cond
  90.0 8.5 %copy-start = (f32[384,384]{1,0:T(8,128)S(1)}, f32[384,384]{1,0:T(8,128)}, u32[]{:S(2)}) copy-start(f32[384,384]{1,0:T(8,128)} %get-tuple-element.184) | copy-start | bytes 1769476 | tf_op jit(solution)/shard_map/cond
  90.0 8.5 %copy-start.48 = (f32[384]{0:T(512)S(1)}, f32[384]{0:T(512)}, u32[]{:S(2)}) copy-start(f32[384]{0:T(512)} %get-tuple-element.139) | copy-start | bytes 4612 | tf_op jit(solution)/shard_map/cond
  90.0 8.5 %copy-start.86 = (f32[384]{0:T(512)S(1)}, f32[384]{0:T(512)}, u32[]{:S(2)}) copy-start(f32[384]{0:T(512)} %copy-done.85) | copy-start | bytes 4612 | tf_op jit(solution)/shard_map/cond
  92.2 7.7 %copy-start.9 = (f32[384,384]{1,0:T(8,128)S(1)}, f32[384,384]{1,0:T(8,128)}, u32[]{:S(2)}) copy-start(f32[384,384]{1,0:T(8,128)} %get-tuple-element.185) | copy-start | bytes 1769476 | tf_op jit(solution)/shard_map/cond
  92.2 7.7 %copy-start.57 = (f32[384]{0:T(512)S(1)}, f32[384]{0:T(512)}, u32[]{:S(2)}) copy-start(f32[384]{0:T(512)} %get-tuple-element.137) | copy-start | bytes 4612 | tf_op jit(solution)/shard_map/cond
  92.2 7.7 %copy-start.95 = (f32[384]{0:T(512)S(1)}, f32[384]{0:T(512)}, u32[]{:S(2)}) copy-start(f32[384]{0:T(512)} %copy-done.94) | copy-start | bytes 4612 | tf_op jit(solution)/shard_map/cond
  106.4 7.1 %copy-start.49 = (f32[384]{0:T(512)S(1)}, f32[384]{0:T(512)}, u32[]{:S(2)}) copy-start(f32[384]{0:T(512)} %get-tuple-element.139) | copy-start | bytes 4612 | tf_op jit(solution)/shard_map/cond
  106.4 7.6 %copy-start.58 = (f32[384]{0:T(512)S(1)}, f32[384]{0:T(512)}, u32[]{:S(2)}) copy-start(f32[384]{0:T(512)} %get-tuple-element.137) | copy-start | bytes 4612 | tf_op jit(solution)/shard_map/cond
  132.0 164.6 %collective-permute-start.14 = (f32[384,6,128]{2,0,1:T(8,128)}, f32[384,6,128]{2,0,1:T(8,128)}, u32[]{:S(2)}, u32[]{:S(2)}) collective-permute-start(f32[384,6,128]{2,0,1:T(8,128)} %get-tuple-element.76), channel_id=1, source_target_pairs={{0,12},{4,16},{8,20},{12,24},{16,28},{20,32},{24,36},{28,40},{32,4... | collective-permute-start | bytes 3538952 | tf_op jit(solution)/shard_map/ppermute | solution.py:14
  135.4 8.3 %copy-start.67 = (f32[384]{0:T(512)}, f32[384]{0:T(512)S(1)}, u32[]{:S(2)}) copy-start(f32[384]{0:T(512)S(1)} %get-tuple-element.124) | copy-start | bytes 4612 | tf_op jit(solution)/shard_map/cond
  151.7 8.4 %copy-start.3 = (f32[384,384]{1,0:T(8,128)S(1)}, f32[384,384]{1,0:T(8,128)}, u32[]{:S(2)}) copy-start(f32[384,384]{1,0:T(8,128)} %get-tuple-element.178) | copy-start | bytes 1769476 | tf_op jit(solution)/shard_map/cond
  151.7 8.4 %copy-start.51 = (f32[384]{0:T(512)S(1)}, f32[384]{0:T(512)}, u32[]{:S(2)}) copy-start(f32[384]{0:T(512)} %get-tuple-element.115) | copy-start | bytes 4612 | tf_op jit(solution)/shard_map/cond
  151.8 8.4 %copy-start.89 = (f32[384]{0:T(512)S(1)}, f32[384]{0:T(512)}, u32[]{:S(2)}) copy-start(f32[384]{0:T(512)} %copy-done.88) | copy-start | bytes 4612 | tf_op jit(solution)/shard_map/cond
  153.9 7.6 %copy-start.12 = (f32[384,384]{1,0:T(8,128)S(1)}, f32[384,384]{1,0:T(8,128)}, u32[]{:S(2)}) copy-start(f32[384,384]{1,0:T(8,128)} %get-tuple-element.179) | copy-start | bytes 1769476 | tf_op jit(solution)/shard_map/cond
  153.9 7.6 %copy-start.60 = (f32[384]{0:T(512)S(1)}, f32[384]{0:T(512)}, u32[]{:S(2)}) copy-start(f32[384]{0:T(512)} %get-tuple-element.113) | copy-start | bytes 4612 | tf_op jit(solution)/shard_map/cond
  153.9 7.6 %copy-start.98 = (f32[384]{0:T(512)S(1)}, f32[384]{0:T(512)}, u32[]{:S(2)}) copy-start(f32[384]{0:T(512)} %copy-done.97) | copy-start | bytes 4612 | tf_op jit(solution)/shard_map/cond
  168.0 7.5 %copy-start.61 = (f32[384]{0:T(512)S(1)}, f32[384]{0:T(512)}, u32[]{:S(2)}) copy-start(f32[384]{0:T(512)} %get-tuple-element.113) | copy-start | bytes 4612 | tf_op jit(solution)/shard_map/cond
  193.2 103.4 %collective-permute-start.9 = (f32[384,6,128]{2,0,1:T(8,128)}, f32[384,6,128]{2,0,1:T(8,128)}, u32[]{:S(2)}, u32[]{:S(2)}) collective-permute-start(f32[384,6,128]{2,0,1:T(8,128)} %get-tuple-element.70), channel_id=1, source_target_pairs={{0,8},{4,12},{8,16},{12,20},{16,24},{20,28},{24,32},{28,36},{32,40... | collective-permute-start | bytes 3538952 | tf_op jit(solution)/shard_map/ppermute | solution.py:14
  214.3 8.5 %copy-start.6 = (f32[384,384]{1,0:T(8,128)S(1)}, f32[384,384]{1,0:T(8,128)}, u32[]{:S(2)}) copy-start(f32[384,384]{1,0:T(8,128)} %get-tuple-element.172) | copy-start | bytes 1769476 | tf_op jit(solution)/shard_map/cond
  214.3 8.5 %copy-start.54 = (f32[384]{0:T(512)S(1)}, f32[384]{0:T(512)}, u32[]{:S(2)}) copy-start(f32[384]{0:T(512)} %get-tuple-element.91) | copy-start | bytes 4612 | tf_op jit(solution)/shard_map/cond
  214.3 8.5 %copy-start.92 = (f32[384]{0:T(512)S(1)}, f32[384]{0:T(512)}, u32[]{:S(2)}) copy-start(f32[384]{0:T(512)} %copy-done.91) | copy-start | bytes 4612 | tf_op jit(solution)/shard_map/cond
  216.5 7.7 %copy-start.15 = (f32[384,384]{1,0:T(8,128)S(1)}, f32[384,384]{1,0:T(8,128)}, u32[]{:S(2)}) copy-start(f32[384,384]{1,0:T(8,128)} %get-tuple-element.173) | copy-start | bytes 1769476 | tf_op jit(solution)/shard_map/cond
  216.5 7.7 %copy-start.63 = (f32[384]{0:T(512)S(1)}, f32[384]{0:T(512)}, u32[]{:S(2)}) copy-start(f32[384]{0:T(512)} %get-tuple-element.89) | copy-start | bytes 4612 | tf_op jit(solution)/shard_map/cond
  216.5 7.7 %copy-start.101 = (f32[384]{0:T(512)S(1)}, f32[384]{0:T(512)}, u32[]{:S(2)}) copy-start(f32[384]{0:T(512)} %copy-done.100) | copy-start | bytes 4612 | tf_op jit(solution)/shard_map/cond
  232.6 7.4 %copy-start.46 = (f32[384]{0:T(512)S(1)}, f32[384]{0:T(512)}, u32[]{:S(2)}) copy-start(f32[384]{0:T(512)} %get-tuple-element.93) | copy-start | bytes 4612 | tf_op jit(solution)/shard_map/cond
  232.7 8.0 %copy-start.55 = (f32[384]{0:T(512)S(1)}, f32[384]{0:T(512)}, u32[]{:S(2)}) copy-start(f32[384]{0:T(512)} %get-tuple-element.91) | copy-start | bytes 4612 | tf_op jit(solution)/shard_map/cond
  232.7 8.5 %copy-start.64 = (f32[384]{0:T(512)S(1)}, f32[384]{0:T(512)}, u32[]{:S(2)}) copy-start(f32[384]{0:T(512)} %get-tuple-element.89) | copy-start | bytes 4612 | tf_op jit(solution)/shard_map/cond
  259.1 7.3 %copy-start.27 = (f32[384,384]{0,1:T(8,128)S(1)}, f32[384,384]{0,1:T(8,128)}, u32[]{:S(2)}) copy-start(f32[384,384]{0,1:T(8,128)} %copy-done.26) | copy-start | bytes 1769476
  259.1 7.3 %copy-start.112 = (f32[384]{0:T(512)S(1)}, f32[384]{0:T(512)}, u32[]{:S(2)}) copy-start(f32[384]{0:T(512)} %copy-done.111) | copy-start | bytes 4612
  259.1 37.5 %collective-permute-start.4 = (f32[384,6,128]{2,0,1:T(8,128)}, f32[384,6,128]{2,0,1:T(8,128)}, u32[]{:S(2)}, u32[]{:S(2)}) collective-permute-start(f32[384,6,128]{2,0,1:T(8,128)} %get-tuple-element.64), channel_id=1, source_target_pairs={{0,4},{4,8},{8,12},{12,16},{16,20},{20,24},{24,28},{28,32},{32,36}... | collective-permute-start | bytes 3538952 | tf_op jit(solution)/shard_map/ppermute | solution.py:14
  261.4 22.1 %copy-start.104 = (f32[384]{0:T(512)S(1)}, f32[384]{0:T(512)}, u32[]{:S(2)}) copy-start(f32[384]{0:T(512)} %copy-done.103) | copy-start | bytes 4612
  261.4 22.1 %copy-start.106 = (f32[384]{0:T(512)S(1)}, f32[384]{0:T(512)}, u32[]{:S(2)}) copy-start(f32[384]{0:T(512)} %copy-done.105) | copy-start | bytes 4612
  261.4 22.1 %copy-start.108 = (f32[384]{0:T(512)S(1)}, f32[384]{0:T(512)}, u32[]{:S(2)}) copy-start(f32[384]{0:T(512)} %copy-done.107) | copy-start | bytes 4612
  261.4 22.1 %copy-start.110 = (f32[384]{0:T(512)S(1)}, f32[384]{0:T(512)}, u32[]{:S(2)}) copy-start(f32[384]{0:T(512)} %copy-done.109) | copy-start | bytes 4612
  261.4 22.1 %copy-start.115 = (f32[384]{0:T(512)S(1)}, f32[384]{0:T(512)}, u32[]{:S(2)}) copy-start(f32[384]{0:T(512)} %fusion.264) | copy-start | bytes 4612
  261.4 22.2 %copy-start.116 = (f32[384]{0:T(512)S(1)}, f32[384]{0:T(512)}, u32[]{:S(2)}) copy-start(f32[384]{0:T(512)} %fusion.266) | copy-start | bytes 4612
  261.5 22.2 %copy-start.117 = (f32[384]{0:T(512)S(1)}, f32[384]{0:T(512)}, u32[]{:S(2)}) copy-start(f32[384]{0:T(512)} %fusion.268) | copy-start | bytes 4612
  261.5 22.2 %copy-start.118 = (f32[384]{0:T(512)S(1)}, f32[384]{0:T(512)}, u32[]{:S(2)}) copy-start(f32[384]{0:T(512)} %fusion.270) | copy-start | bytes 4612
  261.5 22.3 %copy-start.114 = (f32[384,6]{0,1:T(8,128)S(1)}, f32[384,6]{0,1:T(8,128)}, u32[]{:S(2)}) copy-start(f32[384,6]{0,1:T(8,128)} %get-tuple-element.74) | copy-start | bytes 27652
  261.5 26.9 %copy-start.113 = (f32[384,6]{0,1:T(8,128)S(1)}, f32[384,6]{0,1:T(8,128)}, u32[]{:S(2)}) copy-start(f32[384,6]{0,1:T(8,128)} %get-tuple-element.75) | copy-start | bytes 27652
  261.5 34.3 %copy-start.32 = (f32[384,6]{0,1:T(8,128)S(1)}, f32[384,6]{0,1:T(8,128)}, u32[]{:S(2)}) copy-start(f32[384,6]{0,1:T(8,128)} %copy-done.31) | copy-start | bytes 27652
  261.5 34.3 %copy-start.35 = (f32[384,6]{0,1:T(8,128)S(1)}, f32[384,6]{0,1:T(8,128)}, u32[]{:S(2)}) copy-start(f32[384,6]{0,1:T(8,128)} %copy-done.34) | copy-start | bytes 27652
  261.5 35.1 %copy-start.21 = (f32[384,6,128]{2,0,1:T(8,128)S(1)}, f32[384,6,128]{2,0,1:T(8,128)}, u32[]{:S(2)}) copy-start(f32[384,6,128]{2,0,1:T(8,128)} %copy-done.20) | copy-start | bytes 3538948
  261.5 35.1 %copy-start.25 = (f32[384,6,128]{2,0,1:T(8,128)S(1)}, f32[384,6,128]{2,0,1:T(8,128)}, u32[]{:S(2)}) copy-start(f32[384,6,128]{2,0,1:T(8,128)} %copy-done.24) | copy-start | bytes 3538948
  262.5 8.1 %collective-permute-start.7 = (f32[384,6]{0,1:T(8,128)}, f32[384,6]{0,1:T(8,128)S(1)}, u32[]{:S(2)}, u32[]{:S(2)}) collective-permute-start(f32[384,6]{0,1:T(8,128)} %get-tuple-element.68), channel_id=1, source_target_pairs={{0,8},{4,12},{8,16},{12,20},{16,24},{20,28},{24,32},{28,36},{32,40... | collective-permute-start | bytes 27656 | tf_op jit(solution)/shard_map/ppermute | solution.py:14
  264.4 15.1 %collective-permute-start.2 = (f32[384,6]{0,1:T(8,128)}, f32[384,6]{0,1:T(8,128)S(1)}, u32[]{:S(2)}, u32[]{:S(2)}) collective-permute-start(f32[384,6]{0,1:T(8,128)} %get-tuple-element.62), channel_id=1, source_target_pairs={{0,4},{4,8},{8,12},{12,16},{16,20},{20,24},{24,28},{28,32},{32,36}... | collective-permute-start | bytes 27656 | tf_op jit(solution)/shard_map/ppermute | solution.py:14
  270.6 13.2 %collective-permute-start.8 = (f32[384,6]{0,1:T(8,128)}, f32[384,6]{0,1:T(8,128)S(1)}, u32[]{:S(2)}, u32[]{:S(2)}) collective-permute-start(f32[384,6]{0,1:T(8,128)} %get-tuple-element.69), channel_id=1, source_target_pairs={{0,8},{4,12},{8,16},{12,20},{16,24},{20,28},{24,32},{28,36},{32,40... | collective-permute-start | bytes 27656 | tf_op jit(solution)/shard_map/ppermute | solution.py:14
  279.6 8.8 %collective-permute-start.3 = (f32[384,6]{0,1:T(8,128)}, f32[384,6]{0,1:T(8,128)S(1)}, u32[]{:S(2)}, u32[]{:S(2)}) collective-permute-start(f32[384,6]{0,1:T(8,128)} %get-tuple-element.63), channel_id=1, source_target_pairs={{0,4},{4,8},{8,12},{12,16},{16,20},{20,24},{24,28},{28,32},{32,36}... | collective-permute-start | bytes 27656 | tf_op jit(solution)/shard_map/ppermute | solution.py:14
  283.8 7.4 %collective-permute-start.12 = (f32[384,6]{0,1:T(8,128)S(1)}, f32[384,6]{0,1:T(8,128)S(1)}, u32[]{:S(2)}, u32[]{:S(2)}) collective-permute-start(f32[384,6]{0,1:T(8,128)S(1)} %copy-done.114), channel_id=1, source_target_pairs={{0,12},{4,16},{8,20},{12,24},{16,28},{20,32},{24,36},{28,40},{32,4... | collective-permute-start | bytes 27656 | tf_op jit(solution)/shard_map/ppermute | solution.py:14
  288.4 7.4 %collective-permute-start.13 = (f32[384,6]{0,1:T(8,128)S(1)}, f32[384,6]{0,1:T(8,128)S(1)}, u32[]{:S(2)}, u32[]{:S(2)}) collective-permute-start(f32[384,6]{0,1:T(8,128)S(1)} %copy-done.113), channel_id=1, source_target_pairs={{0,12},{4,16},{8,20},{12,24},{16,28},{20,32},{24,36},{28,40},{32,4... | collective-permute-start | bytes 27656 | tf_op jit(solution)/shard_map/ppermute | solution.py:14
  (73 other events, 287.6 us)
where the time goes:
time: 326 us; the launch traced here: 323 us
  matrix products  84.1 us (26%)
  local copies, waits for them, and re-layouts  80.1 us (25%)
  waiting for transfers between devices  58.3 us (18%)
  starting transfers between devices  44.7 us (14%)
  other arithmetic  37.2 us (11%)
  blocking collectives  14.8 us (5%)
    ppermute x15, waiting for transfers between devices, from_behind(): lax.ppermute(value, axis, [(source, source + steps) for source in range(f...  48.7 us
    ppermute x15, starting transfers between devices, from_behind(): lax.ppermute(value, axis, [(source, source + steps) for source in range(f...  37 us
    dot_general x24, matrix products, pair_tile(): lax.dot_general(left, right, (((1,), (1,)), ((), ())), preferred_element_...  34.1 us
    dot_general x24, matrix products, pair_tile(): jnp.dot(weights.astype(jnp.bfloat16), cols_value[:, start:start + DH], pr...  28.2 us
    another operation x21, local copies, waits for them, and re-layouts, pair_tile(): jnp.stack(col_sums, 1)  26.1 us
    reduce_sum x18, other arithmetic, pair_tile(): col_sums.append(jnp.sum(col_weights, axis=0))  23.2 us
    dot_general x18, matrix products, pair_tile(): lax.dot_general(col_weights.astype(jnp.bfloat16), rows_value[:, start:sta...  21.8 us
    all_to_all x1, blocking collectives, local(): lax.all_to_all(attended, 'head', split_axis=0, concat_axis=1, tiled=True)  14.8 us
  transfers between devices with their start and end apart: 17, of which 9 were waited for; matrix products, arithmetic and copies ran while one was open for 56% of the time, Pallas kernels for 0%

commit v1 on v0

v1 whole, which is shorter than its diff:
```python
import functools
import math

import jax
import jax.numpy as jnp
from jax import lax
from jax.experimental import pallas as pl
from jax.experimental.pallas import tpu as pltpu
from jax.sharding import PartitionSpec as P

MESH = pl.DeviceIdType.MESH
DH = 128
PLANE = 8
REACH = 3
SPAN = 2 * REACH + 1
SLOTS = PLANE + 2 * REACH
COLS = 6
DEAD = 1e30
LOG2 = math.log2(math.e) / math.sqrt(DH)


def rows_of(slot, tok):
    return pl.ds(pl.multiple_of(slot * tok, tok), tok)


def wait_bytes(ref, sem):
    pltpu.make_async_copy(ref, ref, sem).wait()


def kernel(
    planes,
    qk_ref,
    value_ref,
    mask_ref,
    out_ref,
    kbuf,
    vbuf,
    mbuf,
    mine,
    pbuf,
    sbuf,
    obuf,
    k_sent,
    v_sent,
    m_sent,
    o_sent,
    halo_sent,
    k_got,
    v_got,
    m_got,
    o_got,
):
    part = qk_ref.shape[0]
    tok = 4 * part
    frame, x = lax.axis_index("frame"), lax.axis_index("head")
    z, phi = frame // PLANE, frame % PLANE
    base = frame - phi
    own_shift = 2 * (x % 2)
    seat = (phi - own_shift + PLANE) % PLANE
    active = seat % 4 != 3
    head = COLS * x + seat - seat // 4
    has_low, has_high = z > 0, z < planes - 1

    def place(x_to, j):
        return (j + j // 3 + 2 * (x_to % 2)) % PLANE

    barrier = pltpu.get_barrier_semaphore()

    def greet(i, c):
        f_to, x_to = i // 4, i % 4

        @pl.when(jnp.logical_or(f_to != phi, x_to != x))
        def _():
            pl.semaphore_signal(barrier, 1, device_id=(base + f_to, x_to), device_id_type=MESH)

        return c

    lax.fori_loop(0, 4 * PLANE, greet, 0)

    @pl.when(has_low)
    def _():
        pl.semaphore_signal(barrier, 1, device_id=(frame - PLANE, x), device_id_type=MESH)

    @pl.when(has_high)
    def _():
        pl.semaphore_signal(barrier, 1, device_id=(frame + PLANE, x), device_id_type=MESH)

    row = lax.broadcasted_iota(jnp.int32, mine.shape, 0)
    picked = jnp.where(row == 0, mask_ref[0, 0], jnp.where(row == 1, mask_ref[0, 1], mask_ref[0, 2]))
    mine[...] = jnp.where(picked == 1, 0.0, DEAD).astype(jnp.float32)
    vbuf[:, DH:] = jnp.ones((SLOTS * tok, DH), jnp.bfloat16)

    @pl.when(jnp.logical_not(has_low))
    def _():
        kbuf[: REACH * tok, :] = jnp.zeros((REACH * tok, DH), jnp.bfloat16)
        vbuf[: REACH * tok, :DH] = jnp.zeros((REACH * tok, DH), jnp.bfloat16)
        for s in range(REACH):
            mbuf[s] = jnp.full(mine.shape, DEAD, jnp.float32)

    @pl.when(jnp.logical_not(has_high))
    def _():
        kbuf[(PLANE + REACH) * tok :, :] = jnp.zeros((REACH * tok, DH), jnp.bfloat16)
        vbuf[(PLANE + REACH) * tok :, :DH] = jnp.zeros((REACH * tok, DH), jnp.bfloat16)

    greeted = 4 * PLANE - 1 + has_low.astype(jnp.int32) + has_high.astype(jnp.int32)
    pl.semaphore_wait(barrier, greeted)

    def scatter(src, dst_of, sent, got):
        def step(i, c):
            x_to = (x + i) % 4
            j = (i // 4 + phi) % COLS
            f_to = place(x_to, j)
            columns = pl.ds(pl.multiple_of((COLS * x_to + j) * DH, DH), DH)
            here = jnp.logical_and(f_to == phi, x_to == x)
            dst = dst_of(pl.ds(pl.multiple_of((REACH + phi) * tok + part * x, part), part))

            @pl.when(here)
            def _():
                pltpu.make_async_copy(src.at[:, columns], dst, got.at[REACH + phi]).start()

            @pl.when(jnp.logical_not(here))
            def _():
                pltpu.make_async_remote_copy(
                    src_ref=src.at[:, columns],
                    dst_ref=dst,
                    send_sem=sent,
                    recv_sem=got.at[REACH + phi],
                    device_id=(base + f_to, x_to),
                    device_id_type=MESH,
                ).start()

            return c

        lax.fori_loop(0, 4 * COLS, step, 0)

    def k_at(rows):
        return kbuf.at[rows, :]

    def v_at(rows):
        return vbuf.at[rows, pl.ds(0, DH)]

    def give_mask(j, c):
        f_to = place(x, j)

        @pl.when(f_to == phi)
        def _():
            pltpu.make_async_copy(mine, mbuf.at[REACH + phi], m_got.at[REACH + phi]).start()

        @pl.when(f_to != phi)
        def _():
            pltpu.make_async_remote_copy(
                src_ref=mine,
                dst_ref=mbuf.at[REACH + phi],
                send_sem=m_sent,
                recv_sem=m_got.at[REACH + phi],
                device_id=(base + f_to, x),
                device_id_type=MESH,
            ).start()

        return c

    scatter(qk_ref, k_at, k_sent, k_got)
    lax.fori_loop(0, COLS, give_mask, 0)
    scatter(value_ref, v_at, v_sent, v_got)

    def up(ref_at, got, n, start):
        return pltpu.make_async_remote_copy(
            src_ref=ref_at(rows_of(REACH + PLANE - 1 - n, tok)),
            dst_ref=ref_at(rows_of(REACH - 1 - n, tok)),
            send_sem=halo_sent.at[start + n],
            recv_sem=got.at[REACH - 1 - n],
            device_id=(frame + PLANE, x),
            device_id_type=MESH,
        )

    def down(ref_at, got, n, start):
        return pltpu.make_async_remote_copy(
            src_ref=ref_at(rows_of(REACH + n, tok)),
            dst_ref=ref_at(rows_of(REACH + PLANE + n, tok)),
            send_sem=halo_sent.at[start + n],
            recv_sem=got.at[REACH + PLANE + n],
            device_id=(frame - PLANE, x),
            device_id_type=MESH,
        )

    def mask_up(n):
        return pltpu.make_async_remote_copy(
            src_ref=mbuf.at[REACH + PLANE - 1 - n],
            dst_ref=mbuf.at[REACH - 1 - n],
            send_sem=halo_sent.at[12 + n],
            recv_sem=m_got.at[REACH - 1 - n],
            device_id=(frame + PLANE, x),
            device_id_type=MESH,
        )

    def pass_on(ref_at, got, first):
        for n in range(REACH):
            wait_bytes(ref_at(rows_of(REACH + PLANE - 1 - n, tok)), got.at[REACH + PLANE - 1 - n])

            @pl.when(has_high)
            def _():
                up(ref_at, got, n, first).start()

            wait_bytes(ref_at(rows_of(REACH + n, tok)), got.at[REACH + n])

            @pl.when(has_low)
            def _():
                down(ref_at, got, n, first + REACH).start()

        for n in range(REACH, PLANE - REACH):
            wait_bytes(ref_at(rows_of(REACH + n, tok)), got.at[REACH + n])

    def frame_at(i):
        return jnp.where(i % 2 == 0, PLANE // 2 - 1 - i // 2, PLANE // 2 + i // 2)

    def wait_halo(i, ref_at, got):
        f = frame_at(i)
        low = f < PLANE // 2
        slot = jnp.where(low, f, f + 2 * REACH)

        @pl.when(jnp.logical_and(i >= 2, jnp.where(low, has_low, has_high)))
        def _():
            wait_bytes(ref_at(rows_of(slot, tok)), got.at[slot])

    def weigh(f):
        q = kbuf[rows_of(f + REACH, tok), :]
        bias = []
        for g in range(SPAN):
            k = g - REACH
            if k < 0:
                bias.append(mbuf[REACH + f + k, pl.ds(-k - 1, 1), :])
            elif k == 0:
                bias.append(None)
            else:
                listed = mbuf[REACH + f, pl.ds(k - 1, 1), :]
                bias.append(jnp.where(jnp.logical_or(has_high, f + k < PLANE), listed, DEAD))
        best = None
        for g in range(SPAN):
            k = kbuf[rows_of(f + g, tok), :]
            s = lax.dot_general(q, k, (((1,), (1,)), ((), ())), preferred_element_type=jnp.float32)
            if g == REACH:
                first = lax.broadcasted_iota(jnp.int32, s.shape, 0)
                second = lax.broadcasted_iota(jnp.int32, s.shape, 1)
                s = jnp.where(first == second, -DEAD, s)
            sbuf[:, g * tok : (g + 1) * tok] = s
            t = functools.reduce(jnp.maximum, [s[:, c : c + DH] for c in range(0, tok, DH)])
            if g != REACH:
                t = t - bias[g]
            best = t if best is None else jnp.maximum(best, t)
        best = jnp.broadcast_to(jnp.max(best, axis=1, keepdims=True) * LOG2, (tok, DH))
        for g in range(SPAN):
            less = best if g == REACH else best + bias[g]
            for c in range(g * tok, (g + 1) * tok, DH):
                pbuf[f, :, c : c + DH] = jnp.exp2(sbuf[:, c : c + DH] * LOG2 - less).astype(jnp.bfloat16)

    def give_out(f, x_to, here):
        rows = pl.ds(pl.multiple_of(f * tok, tok) + x_to * part, part)
        columns = pl.ds(pl.multiple_of(head * DH, DH), DH)

        @pl.when(here)
        def _():
            pltpu.make_async_copy(obuf.at[rows, :], out_ref.at[:, columns], o_got).start()

        @pl.when(jnp.logical_not(here))
        def _():
            pltpu.make_async_remote_copy(
                src_ref=obuf.at[rows, :],
                dst_ref=out_ref.at[:, columns],
                send_sem=o_sent,
                recv_sem=o_got,
                device_id=(base + f, x_to),
                device_id_type=MESH,
            ).start()

    @pl.when(active)
    def _():
        pass_on(k_at, k_got, 0)
        for n in range(PLANE):
            wait_bytes(mbuf.at[REACH + n], m_got.at[REACH + n])
        for n in range(REACH):

            @pl.when(has_high)
            def _():
                mask_up(n).start()

        @pl.when(has_low)
        def _():
            for n in range(REACH):
                wait_bytes(mbuf.at[n], m_got.at[n])

        def scores_step(i, c):
            wait_halo(i, k_at, k_got)
            weigh(frame_at(i))

            @pl.when(i == 4)
            def _():
                pass_on(v_at, v_got, 6)

            return c

        lax.fori_loop(0, PLANE, scores_step, 0)

        def value_step(i, c):
            wait_halo(i, v_at, v_got)
            f = frame_at(i)
            values = vbuf[pl.ds(pl.multiple_of(f * tok, tok), SPAN * tok), :]
            o = jnp.dot(pbuf[f], values, preferred_element_type=jnp.float32)
            obuf[rows_of(f, tok), :] = (o[:, :DH] / o[:, DH:]).astype(jnp.bfloat16)
            for x_to in range(4):
                give_out(f, x_to, jnp.logical_and(f == phi, x == x_to))
            return c

        lax.fori_loop(0, PLANE, value_step, 0)

        wait_bytes(qk_ref.at[:, pl.ds(0, (4 * COLS - 1) * DH)], k_sent)
        wait_bytes(value_ref.at[:, pl.ds(0, (4 * COLS - 1) * DH)], v_sent)
        wait_bytes(mbuf.at[pl.ds(0, COLS - 1)], m_sent)
        wait_bytes(obuf.at[pl.ds(0, (4 * PLANE - 1) * part), :], o_sent)

        @pl.when(has_high)
        def _():
            for n in range(REACH):
                up(k_at, k_got, n, 0).wait_send()
                up(v_at, v_got, n, 6).wait_send()
                mask_up(n).wait_send()

        @pl.when(has_low)
        def _():
            for n in range(REACH):
                down(k_at, k_got, n, REACH).wait_send()
                down(v_at, v_got, n, 6 + REACH).wait_send()

    @pl.when(jnp.logical_not(active))
    def _():
        wait_bytes(qk_ref, k_sent)
        wait_bytes(value_ref, v_sent)
        wait_bytes(mbuf.at[pl.ds(0, COLS)], m_sent)

    wait_bytes(out_ref, o_got)


def solution(mesh):
    planes = mesh.shape["frame"] // PLANE

    def local(qk, value, pair_mask):
        part, width = qk.shape
        tok = 4 * part
        return pl.pallas_call(
            functools.partial(kernel, planes),
            out_shape=jax.ShapeDtypeStruct((part, width), jnp.bfloat16),
            in_specs=[
                pl.BlockSpec(memory_space=pl.ANY),
                pl.BlockSpec(memory_space=pl.ANY),
                pl.BlockSpec(memory_space=pltpu.SMEM),
            ],
            out_specs=pl.BlockSpec(memory_space=pl.ANY),
            scratch_shapes=[
                pltpu.VMEM((SLOTS * tok, DH), jnp.bfloat16),
                pltpu.VMEM((SLOTS * tok, 2 * DH), jnp.bfloat16),
                pltpu.VMEM((PLANE + REACH, 8, DH), jnp.float32),
                pltpu.VMEM((8, DH), jnp.float32),
                pltpu.VMEM((PLANE, tok, SPAN * tok), jnp.bfloat16),
                pltpu.VMEM((tok, SPAN * tok), jnp.float32),
                pltpu.VMEM((PLANE * tok, DH), jnp.bfloat16),
                pltpu.SemaphoreType.DMA,
                pltpu.SemaphoreType.DMA,
                pltpu.SemaphoreType.DMA,
                pltpu.SemaphoreType.DMA,
                pltpu.SemaphoreType.DMA((15,)),
                pltpu.SemaphoreType.DMA((SLOTS,)),
                pltpu.SemaphoreType.DMA((SLOTS,)),
                pltpu.SemaphoreType.DMA((PLANE + REACH,)),
                pltpu.SemaphoreType.DMA,
            ],
            compiler_params=pltpu.CompilerParams(
                collective_id=0, has_side_effects=True, vmem_limit_bytes=52 * 2**20
            ),
        )(qk, value, pair_mask)

    return jax.shard_map(
        local,
        mesh=mesh,
        in_specs=(P(("frame", "head"), None), P(("frame", "head"), None), P("frame", None)),
        out_specs=P(("frame", "head"), None),
        check_vma=False,
    )
```

time: 326 us -> 57.9 us (0.18)
  the two profiles are of different devices: /device:TPU:64 before, /device:TPU:96 now
where the time goes in v1:
time: 57.9 us; the launch traced here: 56.7 us
  Pallas kernels  53.1 us (92%)
  local copies, waits for them, and re-layouts  3.6 us (6%)
    pallas_call x1, Pallas kernels, local(): pl.pallas_call(functools.partial(kernel, planes), out_shape=jax.ShapeDtyp...  53.1 us
    unnamed x7, local copies, waits for them, and re-layouts  3.6 us

profile of v1, /device:TPU:96, one launch (start us, length us, event | category | flops | bytes accessed | tf_op | source)
XLA Modules:
  0.0 56.7 jit_solution(8873978369661752080)
XLA Ops:
  0.0 0.0 copy-start
  0.0 1.1 %copy-done = bf16[96,3072]{1,0:T(8,128)(2,1)S(1)} copy-done((bf16[96,3072]{1,0:T(8,128)(2,1)S(1)}, bf16[96,3072]{1,0:T(8,128)(2,1)}, u32[]{:S(2)}) %copy-start) | copy-done | bytes 589848
  1.1 0.0 copy-start.1
  1.1 1.1 %copy-done.1 = bf16[96,3072]{1,0:T(8,128)(2,1)S(1)} copy-done((bf16[96,3072]{1,0:T(8,128)(2,1)S(1)}, bf16[96,3072]{1,0:T(8,128)(2,1)}, u32[]{:S(2)}) %copy-start.1) | copy-done | bytes 589848
  2.1 0.0 copy-start.2
  2.1 0.7 %copy-done.2 = s32[1,3]{1,0:T(1,128)S(1)} copy-done((s32[1,3]{1,0:T(1,128)S(1)}, s32[1,3]{1,0:T(1,128)}, u32[]{:S(2)}) %copy-start.2) | copy-done | bytes 36
  2.8 53.1 %shard_map.37 = bf16[96,3072]{1,0:T(8,128)(2,1)S(1)} custom-call(bf16[96,3072]{1,0:T(8,128)(2,1)S(1)} %copy-done, bf16[96,3072]{1,0:T(8,128)(2,1)S(1)} %copy-done.1, s32[1,3]{1,0:T(1,128)S(1)} %copy-done.2), custom_call_target="tpu_custom_call" | custom-call | tf_op jit(solution)/shard_map/pallas_call | solution.py:348
  55.9 0.8 %copy.5 = bf16[96,3072]{1,0:T(8,128)(2,1)} copy(bf16[96,3072]{1,0:T(8,128)(2,1)S(1)} %shard_map.37) | data formatting | bytes 1179648
Async XLA Ops:
  0.0 1.1 %copy-start = (bf16[96,3072]{1,0:T(8,128)(2,1)S(1)}, bf16[96,3072]{1,0:T(8,128)(2,1)}, u32[]{:S(2)}) copy-start(bf16[96,3072]{1,0:T(8,128)(2,1)} %qk_ref.1) | copy-start | bytes 1769476
  1.1 1.1 %copy-start.1 = (bf16[96,3072]{1,0:T(8,128)(2,1)S(1)}, bf16[96,3072]{1,0:T(8,128)(2,1)}, u32[]{:S(2)}) copy-start(bf16[96,3072]{1,0:T(8,128)(2,1)} %value_ref.1) | copy-start | bytes 1769476
  2.1 0.7 %copy-start.2 = (s32[1,3]{1,0:T(1,128)S(1)}, s32[1,3]{1,0:T(1,128)}, u32[]{:S(2)}) copy-start(s32[1,3]{1,0:T(1,128)} %mask_ref.1) | copy-start | bytes 40

commit v2 on v1

--- a/solution.py
+++ b/solution.py
@@ -16,6 +16,7 @@
 SLOTS = PLANE + 2 * REACH
 COLS = 6
 DEAD = 1e30
+V_STEP = 5
 LOG2 = math.log2(math.e) / math.sqrt(DH)
 
 
@@ -37,6 +38,7 @@
     vbuf,
     mbuf,
     mine,
+    listed,
     pbuf,
     sbuf,
     obuf,
@@ -44,11 +46,15 @@
     v_sent,
     m_sent,
     o_sent,
-    halo_sent,
+    up_sent,
+    down_sent,
     k_got,
     v_got,
+    k_halo,
+    v_halo,
     m_got,
     o_got,
+    listed_got,
 ):
     part = qk_ref.shape[0]
     tok = 4 * part
@@ -64,6 +70,9 @@
     def place(x_to, j):
         return (j + j // 3 + 2 * (x_to % 2)) % PLANE
 
+    row_copy = pltpu.make_async_copy(mask_ref, listed, listed_got)
+    row_copy.start()
+
     barrier = pltpu.get_barrier_semaphore()
 
     def greet(i, c):
@@ -85,8 +94,9 @@
     def _():
         pl.semaphore_signal(barrier, 1, device_id=(frame + PLANE, x), device_id_type=MESH)
 
+    row_copy.wait()
     row = lax.broadcasted_iota(jnp.int32, mine.shape, 0)
-    picked = jnp.where(row == 0, mask_ref[0, 0], jnp.where(row == 1, mask_ref[0, 1], mask_ref[0, 2]))
+    picked = jnp.where(row == 0, listed[0, 0], jnp.where(row == 1, listed[0, 1], listed[0, 2]))
     mine[...] = jnp.where(picked == 1, 0.0, DEAD).astype(jnp.float32)
     vbuf[:, DH:] = jnp.ones((SLOTS * tok, DH), jnp.bfloat16)
 
@@ -105,33 +115,38 @@
     greeted = 4 * PLANE - 1 + has_low.astype(jnp.int32) + has_high.astype(jnp.int32)
     pl.semaphore_wait(barrier, greeted)
 
-    def scatter(src, dst_of, sent, got):
-        def step(i, c):
-            x_to = (x + i) % 4
-            j = (i // 4 + phi) % COLS
-            f_to = place(x_to, j)
-            columns = pl.ds(pl.multiple_of((COLS * x_to + j) * DH, DH), DH)
-            here = jnp.logical_and(f_to == phi, x_to == x)
-            dst = dst_of(pl.ds(pl.multiple_of((REACH + phi) * tok + part * x, part), part))
-
-            @pl.when(here)
-            def _():
-                pltpu.make_async_copy(src.at[:, columns], dst, got.at[REACH + phi]).start()
-
-            @pl.when(jnp.logical_not(here))
-            def _():
-                pltpu.make_async_remote_copy(
-                    src_ref=src.at[:, columns],
-                    dst_ref=dst,
-                    send_sem=sent,
-                    recv_sem=got.at[REACH + phi],
-                    device_id=(base + f_to, x_to),
-                    device_id_type=MESH,
-                ).start()
-
-            return c
-
-        lax.fori_loop(0, 4 * COLS, step, 0)
+    def offset(i):
+        q, dx = i // 4, i % 4
+        return dx, (q + dx) % 4, (q // 4 + dx) % 2
+
+    def target(i):
+        dx, dy, dc = offset(i)
+        x_to = (x + dx) % 4
+        f_to = (phi // 2 + dy) % 4 * 2 + (phi + dc) % 2
+        seat_to = (f_to + 2 * PLANE - 2 * (x_to % 2)) % PLANE
+        return x_to, f_to, seat_to % 4 != 3, COLS * x_to + seat_to - seat_to // 4
+
+    def origin(i):
+        dx, dy, dc = offset(i)
+        return (x + 4 - dx) % 4, (phi // 2 + 4 - dy) % 4 * 2 + (phi + dc) % 2
+
+    def chunk(f, x_of):
+        return pl.ds(pl.multiple_of((REACH + f) * tok + part * x_of, part), part)
+
+    def parcel(i, src, dst_at, sent, got):
+        x_to, f_to, _, head_to = target(i)
+        return pltpu.make_async_remote_copy(
+            src_ref=src.at[:, pl.ds(pl.multiple_of(head_to * DH, DH), DH)],
+            dst_ref=dst_at(chunk(phi, x)),
+            send_sem=sent,
+            recv_sem=got.at[i],
+            device_id=(base + f_to, x_to),
+            device_id_type=MESH,
+        )
+
+    def keep(src, dst_at, got):
+        columns = pl.ds(pl.multiple_of(head * DH, DH), DH)
+        pltpu.make_async_copy(src.at[:, columns], dst_at(chunk(phi, x)), got.at[0]).start()
 
     def k_at(rows):
         return kbuf.at[rows, :]
@@ -159,68 +174,87 @@
 
         return c
 
-    scatter(qk_ref, k_at, k_sent, k_got)
+    def qk_parcel(i):
+        return parcel(i, qk_ref, k_at, k_sent.at[i], k_got)
+
+    def value_parcel(i):
+        return parcel(i, value_ref, v_at, v_sent, v_got)
+
+    def send_qk(i, c):
+        @pl.when(target(i)[2])
+        def _():
+            qk_parcel(i).start()
+
+        return c
+
+    def pass_on(i, ref_at, got, halo, kind):
+        x_of, f = origin(i)
+        here = ref_at(chunk(f, x_of))
+        wait_bytes(here, got.at[i])
+
+        @pl.when(jnp.logical_and(f >= PLANE - REACH, has_high))
+        def _():
+            pltpu.make_async_remote_copy(
+                src_ref=here,
+                dst_ref=ref_at(chunk(f - PLANE, x_of)),
+                send_sem=up_sent.at[kind],
+                recv_sem=halo.at[f - PLANE + REACH],
+                device_id=(frame + PLANE, x),
+                device_id_type=MESH,
+            ).start()
+
+        @pl.when(jnp.logical_and(f < REACH, has_low))
+        def _():
+            pltpu.make_async_remote_copy(
+                src_ref=here,
+                dst_ref=ref_at(chunk(f + PLANE, x_of)),
+                send_sem=down_sent.at[kind],
+                recv_sem=halo.at[f + REACH],
+                device_id=(frame - PLANE, x),
+                device_id_type=MESH,
+            ).start()
+
+    def exchange(i, c):
+        @pl.when(jnp.logical_and(target(i)[2], i > 0))
+        def _():
+            qk_parcel(i).wait_send()
+            value_parcel(i).start()
+
+        @pl.when(active)
+        def _():
+            pass_on(i, k_at, k_got, k_halo, 0)
+
+        return c
+
     lax.fori_loop(0, COLS, give_mask, 0)
-    scatter(value_ref, v_at, v_sent, v_got)
-
-    def up(ref_at, got, n, start):
-        return pltpu.make_async_remote_copy(
-            src_ref=ref_at(rows_of(REACH + PLANE - 1 - n, tok)),
-            dst_ref=ref_at(rows_of(REACH - 1 - n, tok)),
-            send_sem=halo_sent.at[start + n],
-            recv_sem=got.at[REACH - 1 - n],
-            device_id=(frame + PLANE, x),
-            device_id_type=MESH,
-        )
-
-    def down(ref_at, got, n, start):
-        return pltpu.make_async_remote_copy(
-            src_ref=ref_at(rows_of(REACH + n, tok)),
-            dst_ref=ref_at(rows_of(REACH + PLANE + n, tok)),
-            send_sem=halo_sent.at[start + n],
-            recv_sem=got.at[REACH + PLANE + n],
-            device_id=(frame - PLANE, x),
-            device_id_type=MESH,
-        )
+    lax.fori_loop(1, 4 * PLANE, send_qk, 0)
+
+    @pl.when(active)
+    def _():
+        keep(qk_ref, k_at, k_got)
+        keep(value_ref, v_at, v_got)
 
     def mask_up(n):
         return pltpu.make_async_remote_copy(
             src_ref=mbuf.at[REACH + PLANE - 1 - n],
             dst_ref=mbuf.at[REACH - 1 - n],
-            send_sem=halo_sent.at[12 + n],
+            send_sem=up_sent.at[2 + n],
             recv_sem=m_got.at[REACH - 1 - n],
             device_id=(frame + PLANE, x),
             device_id_type=MESH,
         )
 
-    def pass_on(ref_at, got, first):
-        for n in range(REACH):
-            wait_bytes(ref_at(rows_of(REACH + PLANE - 1 - n, tok)), got.at[REACH + PLANE - 1 - n])
-
-            @pl.when(has_high)
-            def _():
-                up(ref_at, got, n, first).start()
-
-            wait_bytes(ref_at(rows_of(REACH + n, tok)), got.at[REACH + n])
-
-            @pl.when(has_low)
-            def _():
-                down(ref_at, got, n, first + REACH).start()
-
-        for n in range(REACH, PLANE - REACH):
-            wait_bytes(ref_at(rows_of(REACH + n, tok)), got.at[REACH + n])
-
     def frame_at(i):
-        return jnp.where(i % 2 == 0, PLANE // 2 - 1 - i // 2, PLANE // 2 + i // 2)
-
-    def wait_halo(i, ref_at, got):
-        f = frame_at(i)
+        return jnp.where((i + x) % 2 == 0, PLANE // 2 - 1 - i // 2, PLANE // 2 + i // 2)
+
+    def wait_halo(f, ref_at, halo):
         low = f < PLANE // 2
         slot = jnp.where(low, f, f + 2 * REACH)
-
-        @pl.when(jnp.logical_and(i >= 2, jnp.where(low, has_low, has_high)))
-        def _():
-            wait_bytes(ref_at(rows_of(slot, tok)), got.at[slot])
+        index = jnp.where(low, f, f - PLANE + 2 * REACH)
+
+        @pl.when(jnp.where(low, has_low, has_high))
+        def _():
+            wait_bytes(ref_at(rows_of(slot, tok)), halo.at[index])
 
     def weigh(f):
         q = kbuf[rows_of(f + REACH, tok), :]
@@ -232,8 +266,8 @@
             elif k == 0:
                 bias.append(None)
             else:
-                listed = mbuf[REACH + f, pl.ds(k - 1, 1), :]
-                bias.append(jnp.where(jnp.logical_or(has_high, f + k < PLANE), listed, DEAD))
+                given = mbuf[REACH + f, pl.ds(k - 1, 1), :]
+                bias.append(jnp.where(jnp.logical_or(has_high, f + k < PLANE), given, DEAD))
         best = None
         for g in range(SPAN):
             k = kbuf[rows_of(f + g, tok), :]
@@ -272,9 +306,10 @@
                 device_id_type=MESH,
             ).start()
 
+    lax.fori_loop(0, PLANE, exchange, 0)
+
     @pl.when(active)
     def _():
-        pass_on(k_at, k_got, 0)
         for n in range(PLANE):
             wait_bytes(mbuf.at[REACH + n], m_got.at[REACH + n])
         for n in range(REACH):
@@ -283,26 +318,40 @@
             def _():
                 mask_up(n).start()
 
-        @pl.when(has_low)
-        def _():
-            for n in range(REACH):
-                wait_bytes(mbuf.at[n], m_got.at[n])
-
+    lax.fori_loop(PLANE, 4 * PLANE, exchange, 0)
+
+    @pl.when(active)
+    def _():
         def scores_step(i, c):
-            wait_halo(i, k_at, k_got)
-            weigh(frame_at(i))
-
-            @pl.when(i == 4)
+            f = frame_at(i)
+
+            @pl.when(i >= 2)
             def _():
-                pass_on(v_at, v_got, 6)
-
+                wait_halo(f, k_at, k_halo)
+
+            @pl.when(jnp.logical_and(i == 2, has_low))
+            def _():
+                for n in range(REACH):
+                    wait_bytes(mbuf.at[n], m_got.at[n])
+
+            weigh(f)
+
+            def hand_on(n, c):
+                pass_on(n, v_at, v_got, v_halo, 1)
+                return c
+
+            lax.fori_loop(V_STEP * i, jnp.minimum(V_STEP * (i + 1), 4 * PLANE), hand_on, 0)
             return c
 
         lax.fori_loop(0, PLANE, scores_step, 0)
 
         def value_step(i, c):
-            wait_halo(i, v_at, v_got)
             f = frame_at(i)
+
+            @pl.when(i >= 2)
+            def _():
+                wait_halo(f, v_at, v_halo)
+
             values = vbuf[pl.ds(pl.multiple_of(f * tok, tok), SPAN * tok), :]
             o = jnp.dot(pbuf[f], values, preferred_element_type=jnp.float32)
             obuf[rows_of(f, tok), :] = (o[:, :DH] / o[:, DH:]).astype(jnp.bfloat16)
@@ -312,27 +361,24 @@
 
         lax.fori_loop(0, PLANE, value_step, 0)
 
-        wait_bytes(qk_ref.at[:, pl.ds(0, (4 * COLS - 1) * DH)], k_sent)
         wait_bytes(value_ref.at[:, pl.ds(0, (4 * COLS - 1) * DH)], v_sent)
         wait_bytes(mbuf.at[pl.ds(0, COLS - 1)], m_sent)
         wait_bytes(obuf.at[pl.ds(0, (4 * PLANE - 1) * part), :], o_sent)
 
         @pl.when(has_high)
         def _():
+            wait_bytes(kbuf.at[pl.ds(0, REACH * tok), :], up_sent.at[0])
+            wait_bytes(v_at(pl.ds(0, REACH * tok)), up_sent.at[1])
             for n in range(REACH):
-                up(k_at, k_got, n, 0).wait_send()
-                up(v_at, v_got, n, 6).wait_send()
                 mask_up(n).wait_send()
 
         @pl.when(has_low)
         def _():
-            for n in range(REACH):
-                down(k_at, k_got, n, REACH).wait_send()
-                down(v_at, v_got, n, 6 + REACH).wait_send()
+            wait_bytes(kbuf.at[pl.ds(0, REACH * tok), :], down_sent.at[0])
+            wait_bytes(v_at(pl.ds(0, REACH * tok)), down_sent.at[1])
 
     @pl.when(jnp.logical_not(active))
     def _():
-        wait_bytes(qk_ref, k_sent)
         wait_bytes(value_ref, v_sent)
         wait_bytes(mbuf.at[pl.ds(0, COLS)], m_sent)
 
@@ -351,7 +397,7 @@
             in_specs=[
                 pl.BlockSpec(memory_space=pl.ANY),
                 pl.BlockSpec(memory_space=pl.ANY),
-                pl.BlockSpec(memory_space=pltpu.SMEM),
+                pl.BlockSpec(memory_space=pl.ANY),
             ],
             out_specs=pl.BlockSpec(memory_space=pl.ANY),
             scratch_shapes=[
@@ -359,21 +405,26 @@
                 pltpu.VMEM((SLOTS * tok, 2 * DH), jnp.bfloat16),
                 pltpu.VMEM((PLANE + REACH, 8, DH), jnp.float32),
                 pltpu.VMEM((8, DH), jnp.float32),
+                pltpu.SMEM((1, REACH), jnp.int32),
                 pltpu.VMEM((PLANE, tok, SPAN * tok), jnp.bfloat16),
                 pltpu.VMEM((tok, SPAN * tok), jnp.float32),
                 pltpu.VMEM((PLANE * tok, DH), jnp.bfloat16),
+                pltpu.SemaphoreType.DMA((4 * PLANE,)),
                 pltpu.SemaphoreType.DMA,
                 pltpu.SemaphoreType.DMA,
                 pltpu.SemaphoreType.DMA,
+                pltpu.SemaphoreType.DMA((2 + REACH,)),
+                pltpu.SemaphoreType.DMA((2,)),
+                pltpu.SemaphoreType.DMA((4 * PLANE,)),
+                pltpu.SemaphoreType.DMA((4 * PLANE,)),
+                pltpu.SemaphoreType.DMA((2 * REACH,)),
+                pltpu.SemaphoreType.DMA((2 * REACH,)),
+                pltpu.SemaphoreType.DMA((PLANE + REACH,)),
                 pltpu.SemaphoreType.DMA,
-                pltpu.SemaphoreType.DMA((15,)),
-                pltpu.SemaphoreType.DMA((SLOTS,)),
-                pltpu.SemaphoreType.DMA((SLOTS,)),
-                pltpu.SemaphoreType.DMA((PLANE + REACH,)),
                 pltpu.SemaphoreType.DMA,
             ],
             compiler_params=pltpu.CompilerParams(
-                collective_id=0, has_side_effects=True, vmem_limit_bytes=52 * 2**20
+                collective_id=0, has_side_effects=True, vmem_limit_bytes=63 * 2**20
             ),
         )(qk, value, pair_mask)
 

time: 57.9 us -> 54 us (0.933); the launches traced: 56.7 us -> 53.6 us
  local copies, waits for them, and re-layouts: 3.6 us -> 1.92 us
  Pallas kernels: 53.1 us -> 51.7 us
    unnamed x7 -> x1, local copies, waits for them, and re-layouts: 3.6 us -> 1.92 us
    pallas_call x1, Pallas kernels: 53.1 us -> 51.7 us  [local(): pl.pallas_call(functools.partial(kernel, planes), out_shape=jax.ShapeDtyp...]
where the time goes in v2:
time: 54 us; the launch traced here: 53.6 us
  Pallas kernels  51.7 us (96%)
  local copies, waits for them, and re-layouts  1.92 us (4%)
    pallas_call x1, Pallas kernels, local(): pl.pallas_call(functools.partial(kernel, planes), out_shape=jax.ShapeDtyp...  51.7 us
    unnamed x1, local copies, waits for them, and re-layouts  1.92 us

profile of v2, /device:TPU:96, one launch (start us, length us, event | category | flops | bytes accessed | tf_op | source)
XLA Modules:
  0.0 53.6 jit_solution(13783012262762241037)
XLA Ops:
  0.0 51.7 %shard_map.37 = bf16[96,3072]{1,0:T(8,128)(2,1)} custom-call(bf16[96,3072]{1,0:T(8,128)(2,1)} %qk_ref.1, bf16[96,3072]{1,0:T(8,128)(2,1)} %value_ref.1, s32[1,3]{1,0:T(1,128)} %mask_ref.1), custom_call_target="tpu_custom_call" | custom-call | tf_op jit(solution)/shard_map/pallas_call | solution.py:394
  51.7 1.9 %copy.5 = bf16[96,3072]{1,0:T(8,128)(2,1)} copy(bf16[96,3072]{1,0:T(8,128)(2,1)} %shard_map.37) | data formatting | bytes 1179648

commit v3 on v2

--- a/solution.py
+++ b/solution.py
@@ -16,7 +16,9 @@
 SLOTS = PLANE + 2 * REACH
 COLS = 6
 DEAD = 1e30
-V_STEP = 5
+LATE = 2
+PIECES = 3
+V_STEP = 11
 LOG2 = math.log2(math.e) / math.sqrt(DH)
 
 
@@ -346,11 +348,13 @@
         lax.fori_loop(0, PLANE, scores_step, 0)
 
         def value_step(i, c):
-            f = frame_at(i)
-
-            @pl.when(i >= 2)
+            rest = PLANE - LATE
+            f = frame_at(jnp.where(i < LATE, i, LATE + (i - LATE + 2 * ((phi // 2 + x) % 3)) % rest))
+
+            @pl.when(i == LATE)
             def _():
-                wait_halo(f, v_at, v_halo)
+                for n in range(LATE, PLANE):
+                    wait_halo(frame_at(n), v_at, v_halo)
 
             values = vbuf[pl.ds(pl.multiple_of(f * tok, tok), SPAN * tok), :]
             o = jnp.dot(pbuf[f], values, preferred_element_type=jnp.float32)
@@ -385,13 +389,29 @@
     wait_bytes(out_ref, o_got)
 
 
+def hand_over(src, dst, buffer, came, went):
+    step = src.shape[0] // PIECES
+    into, out = [], []
+    for n in range(PIECES):
+        rows = pl.ds(n * step, step)
+        into.append(pltpu.make_async_copy(src.at[rows, :], buffer.at[rows, :], came.at[n]))
+        out.append(pltpu.make_async_copy(buffer.at[rows, :], dst.at[rows, :], went.at[n]))
+    for copy in into:
+        copy.start()
+    for first, second in zip(into, out):
+        first.wait()
+        second.start()
+    for copy in out:
+        copy.wait()
+
+
 def solution(mesh):
     planes = mesh.shape["frame"] // PLANE
 
     def local(qk, value, pair_mask):
         part, width = qk.shape
         tok = 4 * part
-        return pl.pallas_call(
+        made = pl.pallas_call(
             functools.partial(kernel, planes),
             out_shape=jax.ShapeDtypeStruct((part, width), jnp.bfloat16),
             in_specs=[
@@ -427,6 +447,18 @@
                 collective_id=0, has_side_effects=True, vmem_limit_bytes=63 * 2**20
             ),
         )(qk, value, pair_mask)
+        return pl.pallas_call(
+            hand_over,
+            out_shape=jax.ShapeDtypeStruct((part, width), jnp.bfloat16),
+            in_specs=[pl.BlockSpec(memory_space=pl.ANY)],
+            out_specs=pl.BlockSpec(memory_space=pl.ANY),
+            scratch_shapes=[
+                pltpu.VMEM((part, width), jnp.bfloat16),
+                pltpu.SemaphoreType.DMA((PIECES,)),
+                pltpu.SemaphoreType.DMA((PIECES,)),
+            ],
+            compiler_params=pltpu.CompilerParams(vmem_limit_bytes=63 * 2**20),
+        )(made)
 
     return jax.shard_map(
         local,

time: 54 us -> 52.9 us (0.980)
  local copies, waits for them, and re-layouts: 1.92 us -> 0 us
  Pallas kernels: 51.7 us -> 52.7 us
    unnamed x1 -> x0, local copies, waits for them, and re-layouts: 1.92 us -> none
    pallas_call x0 -> x1, Pallas kernels: none -> 1.84 us  [local(): pl.pallas_call(hand_over, out_shape=jax.ShapeDtypeStruct((part, width), j...]
    pallas_call x1, Pallas kernels: 51.7 us -> 50.9 us  [local(): pl.pallas_call(functools.partial(kernel, planes), out_shape=jax.ShapeDtyp...]
where the time goes in v3:
time: 52.9 us; the launch traced here: 52.7 us
  Pallas kernels  52.7 us (100%)
    pallas_call x1, Pallas kernels, local(): pl.pallas_call(functools.partial(kernel, planes), out_shape=jax.ShapeDtyp...  50.9 us
    pallas_call x1, Pallas kernels, local(): pl.pallas_call(hand_over, out_shape=jax.ShapeDtypeStruct((part, width), j...  1.84 us

profile of v3, /device:TPU:96, one launch (start us, length us, event | category | flops | bytes accessed | tf_op | source)
XLA Modules:
  0.0 52.7 jit_solution(2895675903344710019)
XLA Ops:
  0.0 50.9 %shard_map.37.src = bf16[96,3072]{1,0:T(8,128)(2,1)} custom-call(bf16[96,3072]{1,0:T(8,128)(2,1)} %qk_ref.1, bf16[96,3072]{1,0:T(8,128)(2,1)} %value_ref.1, s32[1,3]{1,0:T(1,128)} %mask_ref.1), custom_call_target="tpu_custom_call" | custom-call | tf_op jit(solution)/shard_map/pallas_call | solution.py:414
  50.9 1.8 %shard_map.38 = bf16[96,3072]{1,0:T(8,128)(2,1)} custom-call(bf16[96,3072]{1,0:T(8,128)(2,1)} %shard_map.37.src), custom_call_target="tpu_custom_call" | custom-call | tf_op jit(solution)/shard_map/pallas_call | solution.py:450

commit v4 on v3

--- a/solution.py
+++ b/solution.py
@@ -118,6 +118,7 @@
     pl.semaphore_wait(barrier, greeted)
 
     def offset(i):
+        i = (4 * PLANE - i) % (4 * PLANE)
         q, dx = i // 4, i % 4
         return dx, (q + dx) % 4, (q // 4 + dx) % 2
 
@@ -290,7 +291,7 @@
                 pbuf[f, :, c : c + DH] = jnp.exp2(sbuf[:, c : c + DH] * LOG2 - less).astype(jnp.bfloat16)
 
     def give_out(f, x_to, here):
-        rows = pl.ds(pl.multiple_of(f * tok, tok) + x_to * part, part)
+        rows = pl.ds(pl.multiple_of(f * tok + x_to * part, part), part)
         columns = pl.ds(pl.multiple_of(head * DH, DH), DH)
 
         @pl.when(here)
@@ -359,8 +360,8 @@
             values = vbuf[pl.ds(pl.multiple_of(f * tok, tok), SPAN * tok), :]
             o = jnp.dot(pbuf[f], values, preferred_element_type=jnp.float32)
             obuf[rows_of(f, tok), :] = (o[:, :DH] / o[:, DH:]).astype(jnp.bfloat16)
-            for x_to in range(4):
-                give_out(f, x_to, jnp.logical_and(f == phi, x == x_to))
+            for n in (2, 1, 3, 0):
+                give_out(f, (x + n) % 4, jnp.logical_and(f == phi, n == 0))
             return c
 
         lax.fori_loop(0, PLANE, value_step, 0)

time: 52.9 us -> 52.8 us (level); the launches traced: 52.7 us -> 52.1 us
  Pallas kernels: 52.7 us -> 52.1 us
    pallas_call x1, Pallas kernels: 50.9 us -> 50.2 us  [local(): pl.pallas_call(functools.partial(kernel, planes), out_shape=jax.ShapeDtyp...]
where the time goes in v4:
time: 52.8 us; the launch traced here: 52.1 us
  Pallas kernels  52.1 us (99%)
    pallas_call x1, Pallas kernels, local(): pl.pallas_call(functools.partial(kernel, planes), out_shape=jax.ShapeDtyp...  50.2 us
    pallas_call x1, Pallas kernels, local(): pl.pallas_call(hand_over, out_shape=jax.ShapeDtypeStruct((part, width), j...  1.84 us

profile of v4, /device:TPU:96, one launch (start us, length us, event | category | flops | bytes accessed | tf_op | source)
XLA Modules:
  0.0 52.1 jit_solution(4666040054932009961)
XLA Ops:
  0.0 50.2 %shard_map.37.src = bf16[96,3072]{1,0:T(8,128)(2,1)} custom-call(bf16[96,3072]{1,0:T(8,128)(2,1)} %qk_ref.1, bf16[96,3072]{1,0:T(8,128)(2,1)} %value_ref.1, s32[1,3]{1,0:T(1,128)} %mask_ref.1), custom_call_target="tpu_custom_call" | custom-call | tf_op jit(solution)/shard_map/pallas_call | solution.py:415
  50.2 1.8 %shard_map.38 = bf16[96,3072]{1,0:T(8,128)(2,1)} custom-call(bf16[96,3072]{1,0:T(8,128)(2,1)} %shard_map.37.src), custom_call_target="tpu_custom_call" | custom-call | tf_op jit(solution)/shard_map/pallas_call | solution.py:451
